TPU v7x, 256 devices: a whole 4x4x8 slice. The times are simulated.
256 devices in a mesh: tp: 8 (over z), ep: 32 (over x, y, core).
Axes of the slice: x: 4, y: 4, z: 8, core: 2. Of those that a mesh axis runs over, the one named last changes fastest.
Arguments:
- tokens: bfloat16 [4096, 7168], P('ep', 'tp'), may hold values from -6 to 6
- indices: int32 [4096, 8], P('ep'), may hold values from 0 to 31, all different within a row
- scores: float32 [4096, 8], P('ep'), may hold values from 0.05 to 1
- gate_weight: bfloat16 [32, 7168, 2048], P('ep', None, 'tp'), may hold values from -0.0625 to 0.0625
- up_weight: bfloat16 [32, 7168, 2048], P('ep', None, 'tp'), may hold values from -0.0625 to 0.0625
- down_weight: bfloat16 [32, 7168, 2048], P('ep', 'tp'), may hold values from -0.125 to 0.125
Outputs:
- mixed: bfloat16 [4096, 7168], P('ep', 'tp')
Inputs may be any that keep to these rules, and one draw needn't show every extreme that they name: `indices`: each token names 8 different experts; every expert is named by some token.
All inputs are finite; a program needn't handle non-finite values.
Results may differ from a plain program's by a relative error of at most 0.0057.
Values may be sent and summed in bfloat16 or wider, within the bound.
A program may use at most 128 MiB of HBM per device.

v0:
```python
import jax
import jax.numpy as jnp
from jax import lax
from jax.sharding import PartitionSpec as P


def place(index_block, experts, capacity):
    flattened = index_block.reshape(-1)
    onehot = (flattened[:, None] == jnp.arange(experts, dtype=jnp.int32)[None, :]).astype(jnp.int32)
    earlier = jnp.cumsum(onehot, axis=0) - onehot
    position = jnp.sum(earlier * onehot, axis=1)
    retained = position < capacity
    target = jnp.where(retained, flattened * capacity + position, experts * capacity)
    return (target, retained)


def local(tokens, indices, scores, gate_weight, up_weight, down_weight):
    experts = lax.axis_size("ep")
    tok_rows = tokens.shape[0]
    top_count = indices.shape[1]
    capacity = tok_rows * top_count // experts
    target, retained = place(indices, experts, capacity)
    owner_row = jnp.arange(tok_rows * top_count, dtype=jnp.int32) // top_count
    slot_token = jnp.zeros((experts * capacity,), jnp.int32).at[target].set(owner_row, mode="drop")
    slot_valid = jnp.zeros((experts * capacity,), jnp.int32).at[target].set(1, mode="drop")
    w_gate = gate_weight[0]
    w_up = up_weight[0]
    w_down = down_weight[0]
    whole = lax.all_gather(tokens, "tp", axis=1, tiled=True)
    outgoing = jnp.where(slot_valid[:, None] > 0, whole[slot_token], jnp.zeros((), jnp.bfloat16))
    received = lax.all_to_all(outgoing, "ep", split_axis=0, concat_axis=0, tiled=True)
    gate = jnp.dot(received, w_gate, preferred_element_type=jnp.float32)
    upward = jnp.dot(received, w_up, preferred_element_type=jnp.float32)
    hidden = (jax.nn.silu(gate) * upward).astype(jnp.bfloat16)
    summed = lax.dot_general(
        w_down,
        lax.all_gather(hidden, "tp", axis=1, tiled=True),
        (((1,), (1,)), ((), ())),
        preferred_element_type=jnp.float32,
    )
    results = summed.astype(jnp.bfloat16)
    returned = lax.all_to_all(results, "ep", split_axis=1, concat_axis=1, tiled=True)
    route = 2.5 * scores / jnp.sum(scores, axis=1, keepdims=True)
    route = jnp.where(retained, route.reshape(-1), 0.0)
    picked = jnp.take(returned, jnp.minimum(target, experts * capacity - 1), axis=1).astype(
        jnp.float32
    )
    weighted = picked * route[None, :]
    mixed = jnp.sum(weighted.reshape(weighted.shape[0], tok_rows, top_count), axis=2)
    return mixed.T.astype(jnp.bfloat16)


def solution(mesh):
    placed = (
        P("ep", "tp"),
        P("ep", None),
        P("ep", None),
        P("ep", None, "tp"),
        P("ep", None, "tp"),
        P("ep", "tp", None),
    )
    return jax.shard_map(
        local, mesh=mesh, in_specs=placed, out_specs=P("ep", "tp"), check_vma=False
    )
```

profile of v0, /device:TPU:1, one launch (start us, length us, event | category | flops | bytes accessed | tf_op | source)
XLA Modules:
  0.0 384.3 jit_solution(15744739406032104786)
XLA Ops:
  6.5 0.0 all-gather.3.cloned.1.call-start
  6.5 0.7 all-gather.3.cloned.1.call-update
  7.3 0.0 all-gather.5.cloned.1.call-start
  7.3 0.8 copy.17
  8.1 0.1 eq.29
  8.2 0.1 eq.25
  8.3 9.0 %reduce-window.6 = s32[32,8,128]{2,1,0:T(8,128)S(1)} reduce-window(s32[32,8,128]{2,1,0:T(8,128)S(1)} %fusion.18, s32[]{:T(128)} %constant.24.clone.1), window={size=1x1x128 pad=0_0x0_0x127_0}, to_apply=%region_0.0 | reduce-window | flops 4161536 | bytes 262148 | tf_op jit(solution)/shard_map/reduce-window
  17.3 0.1 slice.12
  17.4 0.1 copy.19
  17.6 0.1 copy.20
  17.7 0.7 broadcast_multiply_fusion
  18.4 0.1 copy.24
  18.5 0.1 mul.47
  18.6 0.1 broadcast_add_fusion
  18.8 4.3 %scatter_custom_fusion.1 = s32[1024]{0:T(1024)S(1)} fusion(s32[1024]{0:T(1024)S(1)} %bitcast.63, s32[1024]{0:T(1024)S(1)} %add_select_fusion, s32[]{:T(128)} %constant.24.clone.1), kind=kCustom, calls=%fused_computation.41 | custom fusion | bytes 4100 | tf_op jit(solution)/shard_map/scatter | solution.py:24
  23.1 4.3 %scatter_custom_fusion = s32[1024]{0:T(1024)S(1)} fusion(s32[1024]{0:T(1024)S(1)} %bitcast.64, s32[1024]{0:T(1024)S(1)} %broadcast.151, s32[]{:T(128)} %constant.24.clone.1), kind=kCustom, calls=%fused_computation.44 | custom fusion | bytes 4100 | tf_op jit(solution)/shard_map/scatter | solution.py:25
  27.4 0.1 broadcast_in_dim.50
  27.5 22.8 %all-gather.3.cloned.1.call-done = bf16[128,7168]{1,0:T(8,128)(2,1)} async-done(((bf16[128,896]{1,0:T(8,128)(2,1)}), bf16[128,7168]{1,0:T(8,128)(2,1)}) %all-gather.3.cloned.1.call-update) | async-done | bytes 1835024 | tf_op jit(solution)/shard_map/all_gather | solution.py:29
  50.3 26.5 %gather_fusion = bf16[1024,7168]{1,0:T(8,128)(2,1)} fusion(bf16[128,7168]{1,0:T(8,128)(2,1)} %all-gather.3.cloned.1.call-done, s32[1024]{0:T(1024)S(1)} %fusion.21), kind=kCustom, calls=%fused_computation | custom fusion | bytes 29364224 | tf_op jit(solution)/shard_map/gather | solution.py:30
  76.8 7.6 %broadcast_select_fusion = bf16[32,32,7168]{2,1,0:T(8,128)(2,1)S(1)} fusion(bf16[32,32,7168]{2,1,0:T(8,128)(2,1)} %bitcast.55, pred[32,32]{1,0:T(8,128)(4,1)S(1)} %broadcast_in_dim.50), kind=kLoop, calls=%fused_computation.4 | loop fusion | flops 7340032 | bytes 29361152 | tf_op jit(solution)/shard_map/jit(_where)/select_n | solution.py:30
  84.4 173.9 %all_to_all.21 = bf16[32,32,7168]{2,1,0:T(8,128)(2,1)S(1)} all-to-all(bf16[32,32,7168]{2,1,0:T(8,128)(2,1)S(1)} %broadcast_select_fusion), channel_id=1, replica_groups=mesh['tp'=8,'ep'=32] {'ep'}, dimensions={0} | all-to-all | bytes 29360128 | tf_op jit(solution)/shard_map/all_to_all | solution.py:31
  258.3 0.0 copy-start.2
  258.3 6.1 %fusion.4 = f32[1024,256]{1,0:T(8,128)S(1)} fusion(bf16[1024,7168]{1,0:T(8,128)(2,1)S(1)} %bitcast.56, bf16[1,7168,256]{2,1,0:T(8,128)(2,1)} %param.9), kind=kOutput, calls=%fused_computation.9 | convolution fusion | flops 3758096384 | bytes 19398656 | tf_op jit(solution)/shard_map/dot_general | solution.py:32
  264.5 0.0 copy-done.2
  264.5 4.8 %fusion.12 = bf16[1024,256]{1,0:T(8,128)(2,1)} fusion(bf16[1024,7168]{1,0:T(8,128)(2,1)S(1)} %bitcast.57, bf16[1,7168,256]{2,1,0:T(8,128)(2,1)S(1)} %copy-done.2, f32[1024,256]{1,0:T(8,128)S(1)} %fusion.4), kind=kOutput, calls=%fused_computation.15 | convolution fusion | flops 3759669248 | bytes 19922944 | tf_op jit(solution)/shard_map/dot_general | solution.py:33
  269.3 0.0 all-gather.5.cloned.1.call-update
  269.3 54.5 %all-gather.5.cloned.1.call-done = bf16[1024,2048]{1,0:T(8,128)(2,1)} async-done(((bf16[1024,256]{1,0:T(8,128)(2,1)}), bf16[1024,2048]{1,0:T(8,128)(2,1)}) %all-gather.5.cloned.1.call-update) | async-done | bytes 4194320 | tf_op jit(solution)/shard_map/all_gather | solution.py:37
  323.8 9.1 %fusion.6 = bf16[1024,896]{1,0:T(8,128)(2,1)} fusion(bf16[1024,2048]{1,0:T(8,128)(2,1)} %all-gather.5.cloned.1.call-done, bf16[1,896,2048]{2,1,0:T(8,128)(2,1)} %param.11), kind=kOutput, calls=%fused_computation.13 | convolution fusion | flops 3759013888 | bytes 9699328 | tf_op jit(solution)/shard_map/dot_general | solution.py:35
  332.9 0.0 copy-start.1
  332.9 0.0 copy-start
  332.9 10.2 %all-to-all-start.1 = ((bf16[896,32,32]{0,2,1:T(8,128)(2,1)}), bf16[896,32,32]{0,2,1:T(8,128)(2,1)S(1)}, u32[]{:S(2)}, u32[]{:S(2)}) async-start(bf16[896,32,32]{0,2,1:T(8,128)(2,1)} %bitcast.58), calls=%async_computation.1 | async-start | bytes 3670016 | tf_op jit(solution)/shard_map/all_to_all | solution.py:42
  343.2 0.1 reduce_sum.32
  343.3 0.0 copy-done.1
  343.3 0.1 copy.25
  343.4 0.0 copy-done
  343.5 0.1 copy.23
  343.6 25.0 %all-to-all-done.1 = bf16[896,32,32]{0,2,1:T(8,128)(2,1)S(1)} async-done(((bf16[896,32,32]{0,2,1:T(8,128)(2,1)}), bf16[896,32,32]{0,2,1:T(8,128)(2,1)S(1)}, u32[]{:S(2)}, u32[]{:S(2)}) %all-to-all-start.1) | async-done | bytes 1835040 | tf_op jit(solution)/shard_map/all_to_all | solution.py:42
  368.6 5.2 %gather_fusion.1 = bf16[1024,896]{1,0:T(8,128)(2,1)} fusion(bf16[896,1024]{0,1:T(8,128)(2,1)S(1)} %bitcast.54, s32[1024]{0:T(1024)S(1)} %broadcast_clamp_fusion), kind=kCustom, calls=%fused_computation.1 | custom fusion | bytes 3674112 | tf_op jit(solution)/shard_map/jit(_take)/gather | solution.py:45
  373.9 3.5 multiply_reduce_fusion
  (15 shorter events, 0.2 us)
Async XLA Ops:
  6.5 43.7 %all-gather.3.cloned.1.call-start = ((), (), s32[]{:S(2)}) async-start(), calls=%async_computation.2 | async-start | bytes 2064384 | tf_op jit(solution)/shard_map/all_gather | solution.py:29
  7.3 316.5 %all-gather.5.cloned.1.call-start = ((), (), s32[]{:S(2)}) async-start(), calls=%async_computation.3 | async-start | bytes 4718592 | tf_op jit(solution)/shard_map/all_gather | solution.py:37
  258.3 6.2 %copy-start.2 = (bf16[1,7168,256]{2,1,0:T(8,128)(2,1)S(1)}, bf16[1,7168,256]{2,1,0:T(8,128)(2,1)}, u32[]{:S(2)}) copy-start(bf16[1,7168,256]{2,1,0:T(8,128)(2,1)} %param.10) | copy-start | bytes 11010052
  332.9 10.4 %copy-start.1 = (f32[128,8]{0,1:T(8,128)S(1)}, f32[128,8]{0,1:T(8,128)}, u32[]{:S(2)}) copy-start(f32[128,8]{0,1:T(8,128)} %param.8) | copy-start | bytes 12292
  332.9 10.5 %copy-start = (s32[128,8]{0,1:T(8,128)S(1)}, s32[128,8]{0,1:T(8,128)}, u32[]{:S(2)}) copy-start(s32[128,8]{0,1:T(8,128)} %param.7) | copy-start | bytes 12292
  332.9 35.7 %all-to-all-start.1 = ((bf16[896,32,32]{0,2,1:T(8,128)(2,1)}), bf16[896,32,32]{0,2,1:T(8,128)(2,1)S(1)}, u32[]{:S(2)}, u32[]{:S(2)}) async-start(bf16[896,32,32]{0,2,1:T(8,128)(2,1)} %bitcast.58), calls=%async_computation.1 | async-start | bytes 3670016 | tf_op jit(solution)/shard_map/all_to_all | solution.py:42
Sparse Core Ops, SparseCore 0:
  9.2 41.0 all-gather.2
  269.4 54.3 all-gather.4
where the time goes:
time: 385 us; the launch traced here: 384 us
  blocking collectives  174 us (45%)
  waiting for transfers between devices  103 us (27%)
  local copies, waits for them, and re-layouts  42.3 us (11%)
  other arithmetic  21.1 us (5%)
  matrix products  20 us (5%)
  between operations  13.6 us (4%)
  starting transfers between devices  10.3 us (3%)
    all_to_all x1, blocking collectives, local(): lax.all_to_all(outgoing, 'ep', split_axis=0, concat_axis=0, tiled=True)  174 us
    all_gather x1, waiting for transfers between devices, local(): lax.all_gather(hidden, 'tp', axis=1, tiled=True)  54.5 us
    gather x1, local copies, waits for them, and re-layouts, local(): whole[slot_token]  26.5 us
    all_to_all x1, waiting for transfers between devices, local(): lax.all_to_all(results, 'ep', split_axis=1, concat_axis=1, tiled=True)  25 us
    all_gather x1, waiting for transfers between devices, local(): whole = lax.all_gather(tokens, 'tp', axis=1, tiled=True)  22.8 us
    all_to_all x1, starting transfers between devices, local(): lax.all_to_all(results, 'ep', split_axis=1, concat_axis=1, tiled=True)  10.2 us
    another operation x3, other arithmetic  9.14 us
    dot_general x1, matrix products, local(): lax.dot_general(w_down, lax.all_gather(hidden, 'tp', axis=1, tiled=True),...  9.11 us
  transfers between devices with their start and end apart: 3, of which 3 were waited for; matrix products, arithmetic and copies ran while one was open for 5% of the time, Pallas kernels for 0%

commit v1 on v0

v1 whole, which is shorter than its diff:
```python
import functools

import jax
import jax.numpy as jnp
from jax import lax
from jax.experimental import pallas as pl
from jax.experimental.pallas import tpu as pltpu
from jax.sharding import PartitionSpec as P

MESH = pl.DeviceIdType.MESH
BF16 = jnp.bfloat16
F32 = jnp.float32
TP = 8
CAP = 32
TOK = 128
FEAT = 896
HID = 256
CHUNKS = 8
BLOCKS = 4
ROWS = BLOCKS * CAP
TOPK = 8
PEERS = CHUNKS * BLOCKS
DIRECT = (0, 2, 6, 4)
TOKEN_SHIFTS = (2, 6, 4)


def dot(a, b):
    return jnp.dot(a, b, preferred_element_type=F32)


def kernel(
    idx_ref, score_ref, tok_in, gate_hbm, up_hbm, down_hbm,
    out_ref,
    w_gate, w_up, w_down, pick, route, tok, outgoing, x, acc_gate, acc_up, hid, res, ret, mix,
    w_sem, tok_send, tok_recv, x_send, x_recv, fwd_send, hid_send, hid_recv, half_recv, ret_send, ret_recv,
):
    z = lax.axis_index("tp")
    e = lax.axis_index("ep")
    ex, ey, ec = lax.div(e, 8), lax.rem(lax.div(e, 2), 4), lax.rem(e, 2)

    def plane(shift):
        return lax.rem(z + shift, TP)

    def peer(c, b, sign):
        dx = lax.div(c, 4) + 2 * (b // 2)
        dy = lax.rem(c, 4) + 2 * (b // 2)
        px = lax.rem(ex + sign * dx + 4, 4)
        py = lax.rem(ey + sign * dy + 8, 4)
        pc = lax.rem(ec + b % 2, 2)
        return (z, (px * 4 + py) * 2 + pc)

    barrier = pltpu.get_barrier_semaphore()

    def greet(c, _):
        for b in range(BLOCKS):
            if b == 0:
                @pl.when(c > 0)
                def _():
                    pl.semaphore_signal(barrier, inc=1, device_id=peer(c, b, 1), device_id_type=MESH)
            else:
                pl.semaphore_signal(barrier, inc=1, device_id=peer(c, b, 1), device_id_type=MESH)
        return 0

    lax.fori_loop(0, CHUNKS, greet, 0)
    for shift in (1, 7, 2, 6, 4):
        pl.semaphore_signal(barrier, inc=1, device_id=(plane(shift), e), device_id_type=MESH)

    weights = [
        pltpu.make_async_copy(gate_hbm, w_gate, w_sem.at[0]),
        pltpu.make_async_copy(up_hbm, w_up, w_sem.at[1]),
        pltpu.make_async_copy(down_hbm, w_down, w_sem.at[2]),
    ]
    for copy in weights:
        copy.start()

    lane = lax.broadcasted_iota(jnp.int32, (TOK, 128), 1)
    row = lax.broadcasted_iota(jnp.int32, (TOK, 128), 0)
    far = 2 * ((lane >> 1) & 1)
    at_x = (ex + ((lane >> 4) & 1) + far) & 3
    at_y = (ey + ((lane >> 2) & 3) + far) & 3
    at_c = (ec + lane) & 1
    expert = jnp.where(lane < PEERS, (at_x * 4 + at_y) * 2 + at_c, -1)
    scores = score_ref[...]
    share = 2.5 * scores / jnp.sum(scores, axis=1, keepdims=True)
    chosen = jnp.zeros((TOK, 128), F32)
    weight = jnp.zeros((TOK, 128), F32)
    for j in range(TOPK):
        hit = idx_ref[:, j : j + 1] == expert
        chosen = jnp.where(hit, 1.0, chosen)
        weight = jnp.where(hit, share[:, j : j + 1], weight)
    before = jnp.where(lane < row, 1.0, 0.0).astype(BF16)
    position = dot(before, chosen.astype(BF16))
    slot = jnp.where(chosen > 0.5, position, -1.0)
    slot_t = slot.T
    place = lax.broadcasted_iota(jnp.int32, (CAP, TOK), 0).astype(F32)
    for k in range(PEERS):
        pick[k // BLOCKS, (k % BLOCKS) * CAP : (k % BLOCKS + 1) * CAP, :] = jnp.where(
            slot_t[k : k + 1, :] == place, 1.0, 0.0
        ).astype(BF16)

    pl.semaphore_wait(barrier, PEERS - 1 + 5)

    def token_copy(n):
        shift = TOKEN_SHIFTS[n]
        return pltpu.make_async_remote_copy(
            src_ref=tok_in, dst_ref=tok.at[n], send_sem=tok_send.at[n], recv_sem=tok_recv.at[n],
            device_id=(plane(TP - shift), e), device_id_type=MESH,
        )

    for n in range(3):
        token_copy(n).start()

    def dispatch(n, c):
        d = DIRECT[n]
        source = tok_in[...] if n == 0 else tok[n - 1]
        outgoing[n, c] = dot(pick[c], source).astype(BF16)
        for b in range(BLOCKS):
            rows = pl.ds(b * CAP, CAP)

            def remote():
                pltpu.make_async_remote_copy(
                    src_ref=outgoing.at[n, c, rows], dst_ref=x.at[d, c, rows],
                    send_sem=x_send.at[n, c], recv_sem=x_recv.at[d, c],
                    device_id=peer(c, b, 1), device_id_type=MESH,
                ).start()

            def own():
                pltpu.make_async_copy(outgoing.at[n, c, rows], x.at[d, c, rows], x_recv.at[d, c]).start()

            if b == 0:
                pl.when(c > 0)(remote)
                pl.when(c == 0)(own)
            else:
                remote()

    def wait(ref, sem):
        pltpu.make_async_copy(ref, ref, sem).wait()

    def arrived(d, c):
        wait(x.at[d, c], x_recv.at[d, c])

    def hand_on(d, c, step, n):
        there = (d - step) % TP
        pltpu.make_async_remote_copy(
            src_ref=x.at[d, c], dst_ref=x.at[there, c],
            send_sem=fwd_send.at[n, c], recv_sem=x_recv.at[there, c],
            device_id=(plane(step % TP), e), device_id_type=MESH,
        ).start()

    def gate_up(c, offsets, gate, up):
        for d in offsets:
            rows = x[d, c]
            at = plane(d)
            g, u = dot(rows, w_gate[at]), dot(rows, w_up[at])
            gate = g if gate is None else gate + g
            up = u if up is None else up + u
        return gate, up

    def hid_copy(src, c, shift, n, half=None):
        rows = pl.ds(0, ROWS) if half is None else pl.ds(half * (ROWS // 2), ROWS // 2)
        recv = half_recv.at[half, c] if half is not None else hid_recv.at[src, c]
        pltpu.make_async_remote_copy(
            src_ref=hid.at[src, c, rows], dst_ref=hid.at[src, c, rows],
            send_sem=hid_send.at[n, c], recv_sem=recv,
            device_id=(plane(shift), e), device_id_type=MESH,
        ).start()

    def hid_wait(src, c):
        wait(hid.at[src, c], hid_recv.at[src, c])

    def first_half(c):
        gate, up = gate_up(c, (0, 2, 6), None, None)
        acc_gate[...] = gate
        acc_up[...] = up

    def second_half(c):
        for d in (4, 1, 7, 3, 5):
            arrived(d, c)
        gate, up = gate_up(c, (4, 1, 7, 3, 5), acc_gate[...], acc_up[...])
        hid[z, c] = (gate / (1.0 + jnp.exp(-gate)) * up).astype(BF16)
        hid_copy(z, c, 1, 0)
        hid_copy(z, c, 7, 1)

    def second_hop(c):
        hid_wait(plane(7), c)
        hid_copy(plane(7), c, 1, 2)
        hid_wait(plane(1), c)
        hid_copy(plane(1), c, 7, 3)

    def third_hop(c):
        hid_wait(plane(6), c)
        hid_copy(plane(6), c, 1, 4)
        hid_copy(plane(6), c, 2, 5, half=0)
        hid_wait(plane(2), c)
        hid_copy(plane(2), c, 7, 6)
        hid_copy(plane(2), c, 6, 7, half=1)

    def ret_block(c, b):
        rows = pl.ds(b * CAP, CAP)

        def remote():
            pltpu.make_async_remote_copy(
                src_ref=res.at[c, rows], dst_ref=ret.at[c, rows],
                send_sem=ret_send.at[c], recv_sem=ret_recv.at[c],
                device_id=peer(c, b, -1), device_id_type=MESH,
            ).start()

        def own():
            pltpu.make_async_copy(res.at[c, rows], ret.at[c, rows], ret_recv.at[c]).start()

        if b == 0:
            pl.when(c > 0)(remote)
            pl.when(c == 0)(own)
        else:
            remote()

    def down(c):
        hid_wait(plane(5), c)
        hid_wait(plane(3), c)
        for half in range(2):
            rows = pl.ds(half * (ROWS // 2), ROWS // 2)
            wait(hid.at[plane(4), c, rows], half_recv.at[half, c])
        total = None
        for s in range(TP):
            part = lax.dot_general(
                hid[s, c], w_down[:, s * HID : (s + 1) * HID], (((1,), (1,)), ((), ())),
                preferred_element_type=F32,
            )
            total = part if total is None else total + part
        res[c] = total.astype(BF16)
        for b in range(BLOCKS):
            ret_block(c, b)

    def combine(c):
        wait(ret.at[c], ret_recv.at[c])
        rows = ret[c]
        mix[...] += dot(route[0, c], rows) + dot(route[1, c], rows) + dot(route[2, c], rows)

    for c in range(3):
        dispatch(0, c)

    high = weight.astype(BF16)
    rest = weight - high.astype(F32)
    middle = rest.astype(BF16)
    low = (rest - middle.astype(F32)).astype(BF16)
    slot_b = slot.astype(BF16)

    def spread(c, _):
        take = jnp.where(row == c * BLOCKS + (lane >> 5), 1.0, 0.0).astype(BF16)
        here = dot(slot_b, take) == (lane & (CAP - 1)).astype(F32)
        for n, part in enumerate((high, middle, low)):
            route[n, c] = jnp.where(here, dot(part, take), 0.0).astype(BF16)
        return 0

    lax.fori_loop(0, CHUNKS, spread, 0)
    mix[...] = jnp.zeros_like(mix)

    for n in (1, 2):
        wait(tok.at[n - 1], tok_recv.at[n - 1])
        dispatch(n, 0)
    for copy in weights:
        copy.wait()

    def step(j, _):
        def at(lag, do):
            c = j - lag
            pl.when(jnp.logical_and(c >= 0, c < CHUNKS))(lambda: do(c))

        def own_slice(c):
            arrived(0, c)
            hand_on(0, c, 1, 0)
            hand_on(0, c, -1, 1)

        def other_slices(c):
            arrived(2, c)
            hand_on(2, c, -1, 2)
            arrived(6, c)
            hand_on(6, c, 1, 3)

        @pl.when(j == 0)
        def _():
            wait(tok.at[2], tok_recv.at[2])

        at(1, second_half)
        at(0, own_slice)
        at(0, lambda c: dispatch(3, c))
        at(1, second_hop)
        at(-3, lambda c: dispatch(0, c))
        at(-1, lambda c: dispatch(1, c))
        at(-1, lambda c: dispatch(2, c))
        at(0, other_slices)
        at(2, down)
        at(0, first_half)
        at(1, third_hop)
        at(3, combine)
        return 0

    lax.fori_loop(0, CHUNKS + 3, step, 0)

    out_ref[...] = mix[...].astype(BF16)

    for n in range(3):
        wait(tok_in, tok_send.at[n])

    def drain(c, _):
        for n in range(4):
            @pl.when(c > 0)
            def _():
                wait(outgoing.at[n, c], x_send.at[n, c])

            @pl.when(c == 0)
            def _():
                part = outgoing.at[n, c, pl.ds(CAP, ROWS - CAP)]
                wait(part, x_send.at[n, c])

            wait(x.at[0, c], fwd_send.at[n, c])
        for n in range(8):
            if n in (5, 7):
                half = hid.at[0, c, pl.ds(0, ROWS // 2)]
                wait(half, hid_send.at[n, c])
            else:
                wait(hid.at[0, c], hid_send.at[n, c])

        @pl.when(c > 0)
        def _():
            wait(res.at[c], ret_send.at[c])

        @pl.when(c == 0)
        def _():
            part = res.at[c, pl.ds(CAP, ROWS - CAP)]
            wait(part, ret_send.at[c])

        return 0

    lax.fori_loop(0, CHUNKS, drain, 0)


def local(tokens, indices, scores, gate_weight, up_weight, down_weight):
    vmem = pl.BlockSpec(memory_space=pltpu.VMEM)
    anywhere = pl.BlockSpec(memory_space=pl.ANY)
    dma = pltpu.SemaphoreType.DMA
    return pl.pallas_call(
        kernel,
        out_shape=jax.ShapeDtypeStruct((TOK, FEAT), BF16),
        in_specs=[vmem, vmem, vmem, anywhere, anywhere, anywhere],
        out_specs=vmem,
        scratch_shapes=[
            pltpu.VMEM((TP, FEAT, HID), BF16),
            pltpu.VMEM((TP, FEAT, HID), BF16),
            pltpu.VMEM((FEAT, TP * HID), BF16),
            pltpu.VMEM((CHUNKS, ROWS, TOK), BF16),
            pltpu.VMEM((3, CHUNKS, TOK, ROWS), BF16),
            pltpu.VMEM((3, TOK, FEAT), BF16),
            pltpu.VMEM((4, CHUNKS, ROWS, FEAT), BF16),
            pltpu.VMEM((TP, CHUNKS, ROWS, FEAT), BF16),
            pltpu.VMEM((ROWS, HID), F32),
            pltpu.VMEM((ROWS, HID), F32),
            pltpu.VMEM((TP, CHUNKS, ROWS, HID), BF16),
            pltpu.VMEM((CHUNKS, ROWS, FEAT), BF16),
            pltpu.VMEM((CHUNKS, ROWS, FEAT), BF16),
            pltpu.VMEM((TOK, FEAT), F32),
            dma((3,)),
            dma((3,)),
            dma((3,)),
            dma((4, CHUNKS)),
            dma((TP, CHUNKS)),
            dma((4, CHUNKS)),
            dma((8, CHUNKS)),
            dma((TP, CHUNKS)),
            dma((2, CHUNKS)),
            dma((CHUNKS,)),
            dma((CHUNKS,)),
        ],
        compiler_params=pltpu.CompilerParams(
            collective_id=0, has_side_effects=True, vmem_limit_bytes=58 * 2**20
        ),
        cost_estimate=pl.CostEstimate(flops=12 * 10**9, bytes_accessed=12 * 10**6, transcendentals=1024 * 256),
    )(
        indices, scores, tokens,
        gate_weight.reshape(TP, FEAT, HID), up_weight.reshape(TP, FEAT, HID), down_weight[0],
    )


def solution(mesh):
    placed = (
        P("ep", "tp"),
        P("ep", None),
        P("ep", None),
        P("ep", None, "tp"),
        P("ep", None, "tp"),
        P("ep", "tp", None),
    )
    return jax.shard_map(
        local, mesh=mesh, in_specs=placed, out_specs=P("ep", "tp"), check_vma=False
    )
```

time: 385 us -> 187 us (0.49)
  Pallas kernels: 0 us -> 181 us
  blocking collectives: 174 us -> 0 us
  waiting for transfers between devices: 103 us -> 0 us
  local copies, waits for them, and re-layouts: 42.3 us -> 4.47 us
  other arithmetic: 21.1 us -> 0 us
  matrix products: 20 us -> 0 us
  between operations: 13.6 us -> 0.01 us
  starting transfers between devices: 10.3 us -> 0 us
    pallas_call x0 -> x1, Pallas kernels: none -> 181 us  [local(): pl.pallas_call(kernel, out_shape=jax.ShapeDtypeStruct((TOK, FEAT), BF16),...]
    all_to_all x1 -> x0, blocking collectives: 174 us -> none  [local(): lax.all_to_all(outgoing, 'ep', split_axis=0, concat_axis=0, tiled=True)]
    all_gather x2 -> x0, waiting for transfers between devices: 77.3 us -> none  [the longest x1 54.5 us: local(): lax.all_gather(hidden, 'tp', axis=1, tiled=True)]
    gather x2 -> x0, local copies, waits for them, and re-layouts: 31.7 us -> none  [the longest x1 26.5 us: local(): whole[slot_token]]
    all_to_all x1 -> x0, waiting for transfers between devices: 25 us -> none  [local(): lax.all_to_all(results, 'ep', split_axis=1, concat_axis=1, tiled=True)]
    dot_general x3 -> x0, matrix products: 20 us -> none  [the longest x1 9.11 us: local(): lax.dot_general(w_down, lax.all_gather(hidden, 'tp', axis=1, tiled=True),...]
    all_to_all x1 -> x0, starting transfers between devices: 10.2 us -> none  [local(): lax.all_to_all(results, 'ep', split_axis=1, concat_axis=1, tiled=True)]
    another operation x3 -> x0, other arithmetic: 9.14 us -> none
  transfers between devices with their start and end apart: 3 -> 0, of which waited for: 3 -> 0; matrix products, arithmetic and copies ran while one was open for 5% -> 0% of each run, Pallas kernels for 0% -> 0%
where the time goes in v1:
time: 187 us; the launch traced here: 186 us
  Pallas kernels  181 us (97%)
  local copies, waits for them, and re-layouts  4.47 us (2%)
    pallas_call x1, Pallas kernels, local(): pl.pallas_call(kernel, out_shape=jax.ShapeDtypeStruct((TOK, FEAT), BF16),...  181 us
    unnamed x3, local copies, waits for them, and re-layouts  4.47 us

profile of v1, /device:TPU:1, one launch (start us, length us, event | category | flops | bytes accessed | tf_op | source)
XLA Modules:
  0.0 185.8 jit_solution(10516910191924882591)
XLA Ops:
  0.0 1.4 copy.7.idx_ref
  1.4 1.4 copy.8.score_ref
  2.8 181.4 %shard_map.64 = bf16[128,896]{1,0:T(8,128)(2,1)} custom-call(s32[128,8]{1,0:T(8,128)} %copy.7.idx_ref, f32[128,8]{1,0:T(8,128)} %copy.8.score_ref, bf16[128,896]{1,0:T(8,128)(2,1)} %tok_in.1, bf16[8,896,256]{2,1,0:T(8,128)(2,1)} %bitcast.3, bf16[8,896,256]{2,1,0:T(8,128)(2,1)} %bitcast.4, bf16[896,2048]{1,0:T(8,128)(2,1)} %bitcast.5), custom_call_target="tpu_custom_call" | custom-call | flops 12000000000 | bytes 12000000 | tf_op jit(solution)/shard_map/pallas_call | solution.py:342
  184.2 1.6 copy.10

commit v2 on v1

--- a/solution.py
+++ b/solution.py
@@ -15,13 +15,32 @@
 TOK = 128
 FEAT = 896
 HID = 256
+TOPK = 8
+PEERS = 32
 CHUNKS = 8
-BLOCKS = 4
+BLOCKS = PEERS // CHUNKS
 ROWS = BLOCKS * CAP
-TOPK = 8
-PEERS = CHUNKS * BLOCKS
-DIRECT = (0, 2, 6, 4)
-TOKEN_SHIFTS = (2, 6, 4)
+HALF = TOK // 2
+DIRECT = (0, 2, 6, 4, 1, 7)
+TOKEN_SHIFTS = (2, 6, 4, 1, 7)
+PLUS = (6, 7)
+MINUS = (6, 7)
+AHEAD_OWN = 4
+AHEAD = 2
+AHEAD_LATE = 1
+AHEAD_HAND = 0
+LAG_HALF = 1
+LAG_HOP2 = 1
+LAG_HOP3 = 1
+LAG_DOWN = 2
+LAG_MIX = 3
+
+
+def among(c, chunks):
+    yes = c < 0
+    for v in chunks:
+        yes = jnp.logical_or(yes, c == v)
+    return yes
 
 
 def dot(a, b):
@@ -32,7 +51,7 @@
     idx_ref, score_ref, tok_in, gate_hbm, up_hbm, down_hbm,
     out_ref,
     w_gate, w_up, w_down, pick, route, tok, outgoing, x, acc_gate, acc_up, hid, res, ret, mix,
-    w_sem, tok_send, tok_recv, x_send, x_recv, fwd_send, hid_send, hid_recv, half_recv, ret_send, ret_recv,
+    w_sem, tok_send, tok_recv, half_send, half_arrive, x_send, x_recv, fwd_send, hid_send, hid_recv, half_recv, ret_send, ret_recv,
 ):
     z = lax.axis_index("tp")
     e = lax.axis_index("ep")
@@ -42,11 +61,11 @@
         return lax.rem(z + shift, TP)
 
     def peer(c, b, sign):
-        dx = lax.div(c, 4) + 2 * (b // 2)
-        dy = lax.rem(c, 4) + 2 * (b // 2)
-        px = lax.rem(ex + sign * dx + 4, 4)
-        py = lax.rem(ey + sign * dy + 8, 4)
-        pc = lax.rem(ec + b % 2, 2)
+        k = c * BLOCKS + b
+        far, core, pair = 2 * (b % 2), lax.rem(lax.div(k, 2), 2), lax.div(k, 4)
+        px = lax.rem(ex + sign * (lax.div(pair, 4) + far) + 8, 4)
+        py = lax.rem(ey + sign * (lax.rem(pair, 4) + far) + 8, 4)
+        pc = lax.rem(ec + core, 2)
         return (z, (px * 4 + py) * 2 + pc)
 
     barrier = pltpu.get_barrier_semaphore()
@@ -75,23 +94,22 @@
 
     lane = lax.broadcasted_iota(jnp.int32, (TOK, 128), 1)
     row = lax.broadcasted_iota(jnp.int32, (TOK, 128), 0)
-    far = 2 * ((lane >> 1) & 1)
-    at_x = (ex + ((lane >> 4) & 1) + far) & 3
-    at_y = (ey + ((lane >> 2) & 3) + far) & 3
-    at_c = (ec + lane) & 1
-    expert = jnp.where(lane < PEERS, (at_x * 4 + at_y) * 2 + at_c, -1)
+    offset = lax.broadcasted_iota(jnp.int32, (PEERS, TOK), 0)
+    far = 2 * (offset & 1)
+    at_x = (ex + (offset >> 4) + far) & 3
+    at_y = (ey + ((offset >> 2) & 3) + far) & 3
+    at_c = (ec + (offset >> 1)) & 1
+    expert = (at_x * 4 + at_y) * 2 + at_c
     scores = score_ref[...]
-    share = 2.5 * scores / jnp.sum(scores, axis=1, keepdims=True)
-    chosen = jnp.zeros((TOK, 128), F32)
-    weight = jnp.zeros((TOK, 128), F32)
+    share = 2.5 * scores / jnp.sum(scores, axis=0, keepdims=True)
+    chosen = jnp.zeros((PEERS, TOK), F32)
+    weight = jnp.zeros((PEERS, TOK), F32)
     for j in range(TOPK):
-        hit = idx_ref[:, j : j + 1] == expert
+        hit = idx_ref[j : j + 1, :] == expert
         chosen = jnp.where(hit, 1.0, chosen)
-        weight = jnp.where(hit, share[:, j : j + 1], weight)
-    before = jnp.where(lane < row, 1.0, 0.0).astype(BF16)
-    position = dot(before, chosen.astype(BF16))
-    slot = jnp.where(chosen > 0.5, position, -1.0)
-    slot_t = slot.T
+        weight = jnp.where(hit, share[j : j + 1, :], weight)
+    before = jnp.where(row < lane, 1.0, 0.0).astype(BF16)
+    slot_t = jnp.where(chosen > 0.5, dot(chosen.astype(BF16), before), -1.0)
     place = lax.broadcasted_iota(jnp.int32, (CAP, TOK), 0).astype(F32)
     for k in range(PEERS):
         pick[k // BLOCKS, (k % BLOCKS) * CAP : (k % BLOCKS + 1) * CAP, :] = jnp.where(
@@ -107,7 +125,15 @@
             device_id=(plane(TP - shift), e), device_id_type=MESH,
         )
 
-    for n in range(3):
+    def relay(n):
+        shift = TOKEN_SHIFTS[n]
+        rows = pl.ds(n * HALF, HALF)
+        return pltpu.make_async_remote_copy(
+            src_ref=tok.at[n, rows], dst_ref=tok.at[2, rows], send_sem=half_send.at[n], recv_sem=half_arrive.at[n],
+            device_id=(plane(TP - shift), e), device_id_type=MESH,
+        )
+
+    for n in (0, 1):
         token_copy(n).start()
 
     def dispatch(n, c):
@@ -170,13 +196,13 @@
 
     def first_half(c):
         gate, up = gate_up(c, (0, 2, 6), None, None)
-        acc_gate[...] = gate
-        acc_up[...] = up
+        acc_gate[lax.rem(c, 4)] = gate
+        acc_up[lax.rem(c, 4)] = up
 
     def second_half(c):
         for d in (4, 1, 7, 3, 5):
             arrived(d, c)
-        gate, up = gate_up(c, (4, 1, 7, 3, 5), acc_gate[...], acc_up[...])
+        gate, up = gate_up(c, (4, 1, 7, 3, 5), acc_gate[lax.rem(c, 4)], acc_up[lax.rem(c, 4)])
         hid[z, c] = (gate / (1.0 + jnp.exp(-gate)) * up).astype(BF16)
         hid_copy(z, c, 1, 0)
         hid_copy(z, c, 7, 1)
@@ -236,9 +262,12 @@
         rows = ret[c]
         mix[...] += dot(route[0, c], rows) + dot(route[1, c], rows) + dot(route[2, c], rows)
 
-    for c in range(3):
+    for c in range(AHEAD_OWN):
         dispatch(0, c)
 
+    pad = TOK - PEERS
+    slot = jnp.concatenate([slot_t, jnp.full((pad, TOK), -1.0, F32)], axis=0).T
+    weight = jnp.concatenate([weight, jnp.zeros((pad, TOK), F32)], axis=0).T
     high = weight.astype(BF16)
     rest = weight - high.astype(F32)
     middle = rest.astype(BF16)
@@ -246,8 +275,10 @@
     slot_b = slot.astype(BF16)
 
     def spread(c, _):
-        take = jnp.where(row == c * BLOCKS + (lane >> 5), 1.0, 0.0).astype(BF16)
-        here = dot(slot_b, take) == (lane & (CAP - 1)).astype(F32)
+        to_row = lax.broadcasted_iota(jnp.int32, (TOK, ROWS), 0)
+        to_lane = lax.broadcasted_iota(jnp.int32, (TOK, ROWS), 1)
+        take = jnp.where(to_row == c * BLOCKS + (to_lane >> 5), 1.0, 0.0).astype(BF16)
+        here = dot(slot_b, take) == (to_lane & (CAP - 1)).astype(F32)
         for n, part in enumerate((high, middle, low)):
             route[n, c] = jnp.where(here, dot(part, take), 0.0).astype(BF16)
         return 0
@@ -255,21 +286,56 @@
     lax.fori_loop(0, CHUNKS, spread, 0)
     mix[...] = jnp.zeros_like(mix)
 
-    for n in (1, 2):
-        wait(tok.at[n - 1], tok_recv.at[n - 1])
-        dispatch(n, 0)
+    for n in (0, 1):
+        wait(tok.at[n], tok_recv.at[n])
+        relay(n).start()
+        if (PLUS, MINUS)[n]:
+            token_copy(n + 3).start()
+        if n == 1:
+            for c in range(AHEAD):
+                dispatch(1, c)
+                dispatch(2, c)
     for copy in weights:
         copy.wait()
+
+    def own_slice(c):
+        arrived(0, c)
+
+        @pl.when(jnp.logical_not(among(c, MINUS)))
+        def _():
+            hand_on(0, c, 1, 0)
+
+        @pl.when(jnp.logical_not(among(c, PLUS)))
+        def _():
+            hand_on(0, c, -1, 1)
+
+    def dispatch_late(c):
+        @pl.when(c == 0)
+        def _():
+            for n in (0, 1):
+                half = tok.at[2, pl.ds(n * HALF, HALF)]
+                wait(half, half_arrive.at[n])
+
+        dispatch(3, c)
+        for n, chunks in ((4, PLUS), (5, MINUS)):
+            if not chunks:
+                continue
+
+            @pl.when(c == chunks[0])
+            def _():
+                wait(tok.at[n - 1], tok_recv.at[n - 1])
+
+            @pl.when(among(c, chunks))
+            def _():
+                dispatch(n, c)
+
+    for c in range(AHEAD_HAND):
+        own_slice(c)
 
     def step(j, _):
         def at(lag, do):
             c = j - lag
             pl.when(jnp.logical_and(c >= 0, c < CHUNKS))(lambda: do(c))
-
-        def own_slice(c):
-            arrived(0, c)
-            hand_on(0, c, 1, 0)
-            hand_on(0, c, -1, 1)
 
         def other_slices(c):
             arrived(2, c)
@@ -277,30 +343,34 @@
             arrived(6, c)
             hand_on(6, c, 1, 3)
 
-        @pl.when(j == 0)
-        def _():
-            wait(tok.at[2], tok_recv.at[2])
-
-        at(1, second_half)
-        at(0, own_slice)
-        at(0, lambda c: dispatch(3, c))
-        at(1, second_hop)
-        at(-3, lambda c: dispatch(0, c))
-        at(-1, lambda c: dispatch(1, c))
-        at(-1, lambda c: dispatch(2, c))
+        def dispatch_ahead(c):
+            dispatch(1, c)
+            dispatch(2, c)
+
+        at(LAG_HALF, second_half)
+        at(-AHEAD_HAND, own_slice)
+        for early in range(AHEAD_LATE):
+            pl.when(j == 0)(functools.partial(dispatch_late, early))
+        at(-AHEAD_LATE, dispatch_late)
+        at(LAG_HOP2, second_hop)
+        at(-AHEAD_OWN, lambda c: dispatch(0, c))
+        at(-AHEAD, dispatch_ahead)
         at(0, other_slices)
-        at(2, down)
+        at(LAG_DOWN, down)
         at(0, first_half)
-        at(1, third_hop)
-        at(3, combine)
+        at(LAG_HOP3, third_hop)
+        at(LAG_MIX, combine)
         return 0
 
-    lax.fori_loop(0, CHUNKS + 3, step, 0)
+    lax.fori_loop(0, CHUNKS + LAG_MIX, step, 0)
 
     out_ref[...] = mix[...].astype(BF16)
 
-    for n in range(3):
+    for n in (0, 1) + ((3,) if PLUS else ()) + ((4,) if MINUS else ()):
         wait(tok_in, tok_send.at[n])
+    for n in (0, 1):
+        half = tok.at[n, pl.ds(n * HALF, HALF)]
+        wait(half, half_send.at[n])
 
     def drain(c, _):
         for n in range(4):
@@ -313,6 +383,16 @@
                 part = outgoing.at[n, c, pl.ds(CAP, ROWS - CAP)]
                 wait(part, x_send.at[n, c])
 
+        for n, other, chunks in ((4, 1, PLUS), (5, 0, MINUS)):
+            @pl.when(among(c, chunks))
+            def _():
+                wait(outgoing.at[n, c], x_send.at[n, c])
+
+            @pl.when(jnp.logical_not(among(c, chunks)))
+            def _():
+                wait(x.at[0, c], fwd_send.at[other, c])
+
+        for n in range(2, 4):
             wait(x.at[0, c], fwd_send.at[n, c])
         for n in range(8):
             if n in (5, 7):
@@ -350,19 +430,21 @@
             pltpu.VMEM((FEAT, TP * HID), BF16),
             pltpu.VMEM((CHUNKS, ROWS, TOK), BF16),
             pltpu.VMEM((3, CHUNKS, TOK, ROWS), BF16),
-            pltpu.VMEM((3, TOK, FEAT), BF16),
-            pltpu.VMEM((4, CHUNKS, ROWS, FEAT), BF16),
+            pltpu.VMEM((5, TOK, FEAT), BF16),
+            pltpu.VMEM((6, CHUNKS, ROWS, FEAT), BF16),
             pltpu.VMEM((TP, CHUNKS, ROWS, FEAT), BF16),
-            pltpu.VMEM((ROWS, HID), F32),
-            pltpu.VMEM((ROWS, HID), F32),
+            pltpu.VMEM((4, ROWS, HID), F32),
+            pltpu.VMEM((4, ROWS, HID), F32),
             pltpu.VMEM((TP, CHUNKS, ROWS, HID), BF16),
             pltpu.VMEM((CHUNKS, ROWS, FEAT), BF16),
             pltpu.VMEM((CHUNKS, ROWS, FEAT), BF16),
             pltpu.VMEM((TOK, FEAT), F32),
             dma((3,)),
-            dma((3,)),
-            dma((3,)),
-            dma((4, CHUNKS)),
+            dma((5,)),
+            dma((5,)),
+            dma((2,)),
+            dma((2,)),
+            dma((6, CHUNKS)),
             dma((TP, CHUNKS)),
             dma((4, CHUNKS)),
             dma((8, CHUNKS)),
@@ -376,7 +458,7 @@
         ),
         cost_estimate=pl.CostEstimate(flops=12 * 10**9, bytes_accessed=12 * 10**6, transcendentals=1024 * 256),
     )(
-        indices, scores, tokens,
+        indices.T, scores.T, tokens,
         gate_weight.reshape(TP, FEAT, HID), up_weight.reshape(TP, FEAT, HID), down_weight[0],
     )
 

time: 187 us -> 173 us (0.925)
  Pallas kernels: 181 us -> 171 us
  local copies, waits for them, and re-layouts: 4.47 us -> 1.65 us
    pallas_call x1, Pallas kernels: 181 us -> 171 us  [local(): pl.pallas_call(kernel, out_shape=jax.ShapeDtypeStruct((TOK, FEAT), BF16),...]
    unnamed x3 -> x1, local copies, waits for them, and re-layouts: 4.47 us -> 1.65 us
where the time goes in v2:
time: 173 us
  Pallas kernels  171 us (99%)
    pallas_call x1, Pallas kernels, local(): pl.pallas_call(kernel, out_shape=jax.ShapeDtypeStruct((TOK, FEAT), BF16),...  171 us

profile of v2, /device:TPU:1, one launch (start us, length us, event | category | flops | bytes accessed | tf_op | source)
XLA Modules:
  0.0 172.8 jit_solution(9082168111969317275)
XLA Ops:
  0.0 171.1 %shard_map.64 = bf16[128,896]{1,0:T(8,128)(2,1)} custom-call(s32[8,128]{1,0:T(8,128)} %bitcast.8, f32[8,128]{1,0:T(8,128)} %bitcast.9, bf16[128,896]{1,0:T(8,128)(2,1)} %tok_in.1, bf16[8,896,256]{2,1,0:T(8,128)(2,1)} %bitcast.5, bf16[8,896,256]{2,1,0:T(8,128)(2,1)} %bitcast.6, bf16[896,2048]{1,0:T(8,128)(2,1)} %bitcast.7), custom_call_target="tpu_custom_call" | custom-call | flops 12000000000 | bytes 12000000 | tf_op jit(solution)/shard_map/pallas_call | solution.py:422
  171.1 1.6 copy.8

commit v3 on v2

--- a/solution.py
+++ b/solution.py
@@ -29,9 +29,11 @@
 AHEAD = 2
 AHEAD_LATE = 1
 AHEAD_HAND = 0
+RAMP = 1
 LAG_HALF = 1
 LAG_HOP2 = 1
 LAG_HOP3 = 1
+LAG_HOP4 = 2
 LAG_DOWN = 2
 LAG_MIX = 3
 
@@ -214,12 +216,20 @@
         hid_copy(plane(1), c, 7, 3)
 
     def third_hop(c):
+        last = c == CHUNKS - 1
         hid_wait(plane(6), c)
         hid_copy(plane(6), c, 1, 4)
-        hid_copy(plane(6), c, 2, 5, half=0)
+        pl.when(last)(lambda: hid_copy(plane(6), c, 2, 5, half=0))
         hid_wait(plane(2), c)
         hid_copy(plane(2), c, 7, 6)
-        hid_copy(plane(2), c, 6, 7, half=1)
+        pl.when(last)(lambda: hid_copy(plane(2), c, 6, 7, half=1))
+
+    def fourth_hop(c):
+        last = c == CHUNKS - 1
+        hid_wait(plane(5), c)
+        pl.when(jnp.logical_not(last))(lambda: hid_copy(plane(5), c, 1, 5, half=0))
+        hid_wait(plane(3), c)
+        pl.when(jnp.logical_not(last))(lambda: hid_copy(plane(3), c, 7, 7, half=1))
 
     def ret_block(c, b):
         rows = pl.ds(b * CAP, CAP)
@@ -241,8 +251,6 @@
             remote()
 
     def down(c):
-        hid_wait(plane(5), c)
-        hid_wait(plane(3), c)
         for half in range(2):
             rows = pl.ds(half * (ROWS // 2), ROWS // 2)
             wait(hid.at[plane(4), c, rows], half_recv.at[half, c])
@@ -333,6 +341,16 @@
         own_slice(c)
 
     def step(j, _):
+        def ahead(lead, do):
+            first = jnp.where(j > RAMP, j + lead + 1, j + lead)
+            end = jnp.where(j >= RAMP, j + lead + 2, j + lead + 1)
+
+            def one(c, _):
+                do(c)
+                return 0
+
+            lax.fori_loop(jnp.minimum(first, CHUNKS), jnp.minimum(end, CHUNKS), one, 0)
+
         def at(lag, do):
             c = j - lag
             pl.when(jnp.logical_and(c >= 0, c < CHUNKS))(lambda: do(c))
@@ -352,9 +370,10 @@
         for early in range(AHEAD_LATE):
             pl.when(j == 0)(functools.partial(dispatch_late, early))
         at(-AHEAD_LATE, dispatch_late)
+        at(LAG_HOP4, fourth_hop)
         at(LAG_HOP2, second_hop)
-        at(-AHEAD_OWN, lambda c: dispatch(0, c))
-        at(-AHEAD, dispatch_ahead)
+        ahead(AHEAD_OWN, lambda c: dispatch(0, c))
+        ahead(AHEAD, dispatch_ahead)
         at(0, other_slices)
         at(LAG_DOWN, down)
         at(0, first_half)

time: 173 us -> 171 us (0.988)
  Pallas kernels: 171 us -> 169 us
    pallas_call x1, Pallas kernels: 171 us -> 169 us  [local(): pl.pallas_call(kernel, out_shape=jax.ShapeDtypeStruct((TOK, FEAT), BF16),...]
where the time goes in v3:
time: 171 us
  Pallas kernels  169 us (99%)
    pallas_call x1, Pallas kernels, local(): pl.pallas_call(kernel, out_shape=jax.ShapeDtypeStruct((TOK, FEAT), BF16),...  169 us

profile of v3, /device:TPU:1, one launch (start us, length us, event | category | flops | bytes accessed | tf_op | source)
XLA Modules:
  0.0 170.9 jit_solution(5741562794221159701)
XLA Ops:
  0.0 169.3 %shard_map.64 = bf16[128,896]{1,0:T(8,128)(2,1)} custom-call(s32[8,128]{1,0:T(8,128)} %bitcast.8, f32[8,128]{1,0:T(8,128)} %bitcast.9, bf16[128,896]{1,0:T(8,128)(2,1)} %tok_in.1, bf16[8,896,256]{2,1,0:T(8,128)(2,1)} %bitcast.5, bf16[8,896,256]{2,1,0:T(8,128)(2,1)} %bitcast.6, bf16[896,2048]{1,0:T(8,128)(2,1)} %bitcast.7), custom_call_target="tpu_custom_call" | custom-call | flops 12000000000 | bytes 12000000 | tf_op jit(solution)/shard_map/pallas_call | solution.py:441
  169.3 1.6 copy.8

commit v4 on v3

--- a/solution.py
+++ b/solution.py
@@ -340,6 +340,51 @@
     for c in range(AHEAD_HAND):
         own_slice(c)
 
+    def drain(c):
+        for n in range(4):
+            @pl.when(c > 0)
+            def _():
+                wait(outgoing.at[n, c], x_send.at[n, c])
+
+            @pl.when(c == 0)
+            def _():
+                part = outgoing.at[n, c, pl.ds(CAP, ROWS - CAP)]
+                wait(part, x_send.at[n, c])
+
+        for n, other, chunks in ((4, 1, PLUS), (5, 0, MINUS)):
+            @pl.when(among(c, chunks))
+            def _():
+                wait(outgoing.at[n, c], x_send.at[n, c])
+
+            @pl.when(jnp.logical_not(among(c, chunks)))
+            def _():
+                wait(x.at[0, c], fwd_send.at[other, c])
+
+        for n in range(2, 4):
+            wait(x.at[0, c], fwd_send.at[n, c])
+        for n in range(8):
+            if n in (5, 7):
+                half = hid.at[0, c, pl.ds(0, ROWS // 2)]
+                wait(half, hid_send.at[n, c])
+            else:
+                wait(hid.at[0, c], hid_send.at[n, c])
+
+        @pl.when(c > 0)
+        def _():
+            wait(res.at[c], ret_send.at[c])
+
+        @pl.when(c == 0)
+        def _():
+            part = res.at[c, pl.ds(CAP, ROWS - CAP)]
+            wait(part, ret_send.at[c])
+
+    def drain_tokens():
+        for n in (0, 1) + ((3,) if PLUS else ()) + ((4,) if MINUS else ()):
+            wait(tok_in, tok_send.at[n])
+        for n in (0, 1):
+            half = tok.at[n, pl.ds(n * HALF, HALF)]
+            wait(half, half_send.at[n])
+
     def step(j, _):
         def ahead(lead, do):
             first = jnp.where(j > RAMP, j + lead + 1, j + lead)
@@ -378,60 +423,14 @@
         at(LAG_DOWN, down)
         at(0, first_half)
         at(LAG_HOP3, third_hop)
+        pl.when(j == CHUNKS)(drain_tokens)
+        at(LAG_MIX, drain)
         at(LAG_MIX, combine)
         return 0
 
     lax.fori_loop(0, CHUNKS + LAG_MIX, step, 0)
 
     out_ref[...] = mix[...].astype(BF16)
-
-    for n in (0, 1) + ((3,) if PLUS else ()) + ((4,) if MINUS else ()):
-        wait(tok_in, tok_send.at[n])
-    for n in (0, 1):
-        half = tok.at[n, pl.ds(n * HALF, HALF)]
-        wait(half, half_send.at[n])
-
-    def drain(c, _):
-        for n in range(4):
-            @pl.when(c > 0)
-            def _():
-                wait(outgoing.at[n, c], x_send.at[n, c])
-
-            @pl.when(c == 0)
-            def _():
-                part = outgoing.at[n, c, pl.ds(CAP, ROWS - CAP)]
-                wait(part, x_send.at[n, c])
-
-        for n, other, chunks in ((4, 1, PLUS), (5, 0, MINUS)):
-            @pl.when(among(c, chunks))
-            def _():
-                wait(outgoing.at[n, c], x_send.at[n, c])
-
-            @pl.when(jnp.logical_not(among(c, chunks)))
-            def _():
-                wait(x.at[0, c], fwd_send.at[other, c])
-
-        for n in range(2, 4):
-            wait(x.at[0, c], fwd_send.at[n, c])
-        for n in range(8):
-            if n in (5, 7):
-                half = hid.at[0, c, pl.ds(0, ROWS // 2)]
-                wait(half, hid_send.at[n, c])
-            else:
-                wait(hid.at[0, c], hid_send.at[n, c])
-
-        @pl.when(c > 0)
-        def _():
-            wait(res.at[c], ret_send.at[c])
-
-        @pl.when(c == 0)
-        def _():
-            part = res.at[c, pl.ds(CAP, ROWS - CAP)]
-            wait(part, ret_send.at[c])
-
-        return 0
-
-    lax.fori_loop(0, CHUNKS, drain, 0)
 
 
 def local(tokens, indices, scores, gate_weight, up_weight, down_weight):

time: 171 us -> 171 us (level)
  no operation moved by 1% of the time
where the time goes in v4:
time: 171 us
  Pallas kernels  169 us (99%)
    pallas_call x1, Pallas kernels, local(): pl.pallas_call(kernel, out_shape=jax.ShapeDtypeStruct((TOK, FEAT), BF16),...  169 us

profile of v4, /device:TPU:1, one launch (start us, length us, event | category | flops | bytes accessed | tf_op | source)
XLA Modules:
  0.0 170.7 jit_solution(15886530046424640459)
XLA Ops:
  0.0 169.0 %shard_map.64 = bf16[128,896]{1,0:T(8,128)(2,1)} custom-call(s32[8,128]{1,0:T(8,128)} %bitcast.8, f32[8,128]{1,0:T(8,128)} %bitcast.9, bf16[128,896]{1,0:T(8,128)(2,1)} %tok_in.1, bf16[8,896,256]{2,1,0:T(8,128)(2,1)} %bitcast.5, bf16[8,896,256]{2,1,0:T(8,128)(2,1)} %bitcast.6, bf16[896,2048]{1,0:T(8,128)(2,1)} %bitcast.7), custom_call_target="tpu_custom_call" | custom-call | flops 12000000000 | bytes 12000000 | tf_op jit(solution)/shard_map/pallas_call | solution.py:440
  169.0 1.6 copy.8
